TPU v7x, 32 devices: a whole 2x2x4 slice. The times are simulated.
32 devices in a mesh: seq: 8 (over y, x, core), mp: 4 (over z).
Axes of the slice: x: 2, y: 2, z: 4, core: 2. Of those that a mesh axis runs over, the one named last changes fastest.
Arguments:
- query_latent: bfloat16 [2048, 1536], P(('seq', 'mp')), may hold values from -6 to 6
- new_kv: bfloat16 [2048, 576], P(('seq', 'mp')), may hold values from -6 to 6
- q_weight: bfloat16 [1536, 24576], P('seq', 'mp'), may hold values from -0.15625 to 0.15625
- q_scales: float32 [12, 192], P(None, 'mp'), may hold values from 0.5 to 2
- kv_weight: bfloat16 [32768, 512], P(('mp', 'seq')), may hold values from -0.5 to 0.5
- kv_scales: float32 [256, 4], P('mp'), may hold values from 0.5 to 2
- kv_gain: float32 [512], replicated, may hold values from 0.1 to 1.9
- pool_latent: bfloat16 [128, 64, 512], P('seq'), may hold values from -64 to 64
- pool_rope: bfloat16 [128, 4096], P('seq'), may hold values from -6 to 6
- page_table: int32 [8, 16], replicated, may hold values from 0 to 127, as said below
- prior_len: int32 [8], replicated, may hold values from 1 to 1024, as said below
Outputs:
- attended: bfloat16 [2048, 16384], P('seq', 'mp')
Inputs may be any that keep to these rules, and one draw needn't show every extreme that they name: `page_table`: pool pages 16 * d to 16 * d + 15 sit on seq device d, and reply r's tokens on seq device r. Every pool page serves exactly one (reply, page) pair. Page j of every reply r lies on device (r + o_j) mod 8 for offsets o_j common to all replies. No device holds more than 2 pages of one reply, and in every draw some device holds exactly 2 pages of each reply. `prior_len`: some reply reaches the most.
All inputs are finite; a program needn't handle non-finite values.
Results may differ from a plain program's by a relative error of at most 0.009.
The roundings to bfloat16 on the way count: a program that leaves them out, or rounds other values in their place, can miss the bound.
Values may be sent and summed in bfloat16 or wider, within the bound.
A program may use at most 192 MiB of HBM per device.

v0:
```python
import math

import jax
import jax.numpy as jnp
from jax import lax
from jax.sharding import PartitionSpec as P

NOPE = 128
ROPE = 64
VDIM = 128
LATENT = 512
BLOCK = 128


NORM_EPS = 1e-06


def rope_tables(positions):
    half_width = ROPE // 2
    frequency = 10000.0 ** (-2.0 * jnp.arange(half_width, dtype=jnp.float32) / ROPE)
    angles = positions.astype(jnp.float32)[:, None] * frequency[None, :]
    return (jnp.cos(angles), jnp.sin(angles))


def rotate(values, cosine, sine_table):
    half_width = values.shape[-1] // 2
    leading = values[..., :half_width]
    trailing = values[..., half_width:]
    return jnp.concatenate(
        [leading * cosine - trailing * sine_table, trailing * cosine + leading * sine_table],
        axis=-1,
    )


def dequantize_rows(values, scale_grid, first_row):
    row_ids = (first_row + jnp.arange(values.shape[0], dtype=jnp.int32)) // BLOCK
    row_pick = (
        row_ids[:, None] == jnp.arange(scale_grid.shape[0], dtype=jnp.int32)[None, :]
    ).astype(jnp.float32)
    per_row = jnp.sum(row_pick[:, :, None] * scale_grid[None, :, :], axis=1)
    factors = jnp.repeat(per_row, BLOCK, axis=1)
    return (values.astype(jnp.float32) * factors).astype(jnp.bfloat16)


def add_rows(query_rows, weight_rows, offset, scale_grid):
    dense_rows = dequantize_rows(weight_rows, scale_grid, offset)
    return jnp.dot(query_rows, dense_rows, preferred_element_type=jnp.float32)


def body(
    query_latent,
    new_kv,
    q_weight,
    q_scales,
    kv_weight,
    kv_scales,
    kv_gain,
    pool_latent,
    pool_rope,
    page_table,
    prior_len,
):
    seq_count = lax.axis_size("seq")
    own_index = lax.axis_index("seq")
    query_rows, new_rows = (
        lax.all_gather(query_latent, "mp", axis=0, tiled=True),
        lax.all_gather(new_kv, "mp", axis=0, tiled=True),
    )
    tok_rows = query_rows.shape[0]
    q_full = add_rows(
        query_rows, lax.all_gather(q_weight, "seq", axis=0, tiled=True), jnp.int32(0), q_scales
    )
    kv_panel = lax.all_gather(kv_weight, "seq", axis=0, tiled=True)
    head_count = kv_panel.shape[0] // (NOPE + VDIM)
    kv_dense = dequantize_rows(kv_panel, kv_scales, 0).reshape(head_count, NOPE + VDIM, LATENT)
    key_weight = kv_dense[:, :NOPE, :]
    value_weight = kv_dense[:, NOPE:, :]
    queries = q_full.astype(jnp.bfloat16).reshape(tok_rows, head_count, NOPE + ROPE)
    length = lax.dynamic_index_in_dim(prior_len, own_index, 0, keepdims=False)
    positions = length + jnp.arange(tok_rows, dtype=jnp.int32)
    cosine, sine_table = rope_tables(positions)
    query_rope = rotate(
        queries[:, :, NOPE:].astype(jnp.float32), cosine[:, None, :], sine_table[:, None, :]
    ).astype(jnp.bfloat16)
    query_lat = jnp.einsum(
        "thd,hdc->thc", queries[:, :, :NOPE], key_weight, preferred_element_type=jnp.float32
    ).astype(jnp.bfloat16)
    latent_part = new_rows[:, :LATENT].astype(jnp.float32)
    inv_rms = lax.rsqrt(jnp.mean(latent_part * latent_part, axis=-1, keepdims=True) + NORM_EPS)
    new_lat = (latent_part * inv_rms * kv_gain[None, :]).astype(jnp.bfloat16)
    new_rope = rotate(new_rows[:, LATENT:].astype(jnp.float32), cosine, sine_table).astype(
        jnp.bfloat16
    )
    page_count = page_table.shape[1]
    pool_count = pool_latent.shape[0]
    page_len = pool_latent.shape[1]
    holders = page_table // pool_count
    pool_slots = page_table % pool_count
    earlier = jnp.arange(page_count)[None, :] < jnp.arange(page_count)[:, None]
    same_holder = holders[:, :, None] == holders[:, None, :]
    page_ranks = jnp.sum(jnp.where(same_holder & earlier[None], 1, 0), axis=2)
    capacity = (page_count + seq_count - 1) // seq_count
    wanted = (holders[:, None, :] == own_index) & (
        page_ranks[:, None, :] == jnp.arange(capacity)[None, :, None]
    )
    send_slot = jnp.sum(jnp.where(wanted, pool_slots[:, None, :], 0), axis=2).reshape(-1)
    send_lat = pool_latent[send_slot].reshape(seq_count, capacity, page_len, LATENT)
    send_rope = pool_rope[send_slot].reshape(seq_count, capacity, pool_rope.shape[1])
    got_lat, got_rope = (
        lax.all_to_all(send_lat, "seq", split_axis=0, concat_axis=0, tiled=True),
        lax.all_to_all(send_rope, "seq", split_axis=0, concat_axis=0, tiled=True),
    )
    own_holders = lax.dynamic_index_in_dim(holders, own_index, 0, keepdims=False)
    own_ranks = lax.dynamic_index_in_dim(page_ranks, own_index, 0, keepdims=False)
    where_from = own_holders * capacity + own_ranks
    prior_keys = page_count * page_len
    prior_lat = got_lat.reshape(seq_count * capacity, page_len, LATENT)[where_from].reshape(
        prior_keys, LATENT
    )
    prior_rope = got_rope.reshape(seq_count * capacity, pool_rope.shape[1])[where_from].reshape(
        prior_keys, ROPE
    )
    score_scale = 1.0 / math.sqrt(NOPE + ROPE)

    def score_keys(keys_lat, keys_rope):
        lat_part = jnp.einsum(
            "thc,kc->htk", query_lat, keys_lat, preferred_element_type=jnp.float32
        )
        rope_part = jnp.einsum(
            "thr,kr->htk", query_rope, keys_rope, preferred_element_type=jnp.float32
        )
        return (lat_part + rope_part) * score_scale

    prior_scores = score_keys(prior_lat, prior_rope)
    prior_index = jnp.arange(prior_keys, dtype=jnp.int32)
    prior_scores = jnp.where(prior_index[None, None, :] < length, prior_scores, -jnp.inf)
    new_scores = score_keys(new_lat, new_rope)
    causal = jnp.arange(tok_rows)[None, :] <= jnp.arange(tok_rows)[:, None]
    new_scores = jnp.where(causal[None], new_scores, -jnp.inf)
    scores = jnp.concatenate([prior_scores, new_scores], axis=2)
    row_max = jnp.max(scores, axis=2, keepdims=True)
    exponent = jnp.exp(scores - row_max)
    weights = (exponent / jnp.sum(exponent, axis=2, keepdims=True)).astype(jnp.bfloat16)
    keys_lat = jnp.concatenate([prior_lat, new_lat], axis=0)
    mixed = jnp.einsum("htk,kc->thc", weights, keys_lat, preferred_element_type=jnp.float32).astype(
        jnp.bfloat16
    )
    attended = jnp.einsum(
        "thc,hvc->thv", mixed, value_weight, preferred_element_type=jnp.float32
    ).astype(jnp.bfloat16)
    return attended.reshape(tok_rows, head_count * VDIM)


def solution(mesh):
    in_specs = (
        P(("seq", "mp"), None),
        P(("seq", "mp"), None),
        P("seq", "mp"),
        P(None, "mp"),
        P(("mp", "seq"), None),
        P("mp", None),
        P(),
        P("seq", None, None),
        P("seq", None),
        P(),
        P(),
    )
    out_specs = P("seq", "mp")
    return jax.shard_map(body, mesh=mesh, in_specs=in_specs, out_specs=out_specs, check_vma=False)
```

profile of v0, /device:TPU:0, one launch (start us, length us, event | category | flops | bytes accessed | tf_op | source)
XLA Modules:
  0.0 328.8 jit_solution(11849190574955136682)
XLA Ops:
  10.1 1.7 gather_fusion.2
  12.5 5.2 %all-to-all-start.1 = ((bf16[8,2,4096]{2,1,0:T(2,128)(2,1)}), bf16[8,2,4096]{2,1,0:T(2,128)(2,1)S(1)}, u32[]{:S(2)}, u32[]{:S(2)}) async-start(bf16[8,2,4096]{2,1,0:T(2,128)(2,1)} %reshape.281), calls=%async_computation.1 | async-start | bytes 262144 | tf_op jit(solution)/shard_map/all_to_all | solution.py:111
  17.7 14.9 %all_gather.13 = bf16[256,576]{1,0:T(8,128)(2,1)S(1)} all-gather(bf16[64,576]{1,0:T(8,128)(2,1)} %param.12), channel_id=1, replica_groups=mesh['seq'=8,'mp'=4] {'mp'}, dimensions={0}, use_global_device_ids=true | all-gather | bytes 368640 | tf_op jit(solution)/shard_map/all_gather | solution.py:67
  32.7 1.2 dynamic_slice.13
  33.9 1.2 add_convert_fusion.2
  35.1 1.2 iota_compare_fusion.5
  36.5 1.0 multiply_reduce_fusion.1
  38.2 0.9 multiply_reduce_fusion
  39.1 1.6 gather_fusion
  40.8 3.9 %all-to-all-start = ((bf16[8,2,64,512]{3,2,1,0:T(8,128)(2,1)}), bf16[8,2,64,512]{3,2,1,0:T(8,128)(2,1)S(1)}, u32[]{:S(2)}, u32[]{:S(2)}) async-start(bf16[8,2,64,512]{3,2,1,0:T(8,128)(2,1)} %bitcast.2), calls=%async_computation | async-start | bytes 2097152 | tf_op jit(solution)/shard_map/all_to_all | solution.py:110
  44.7 2.6 copy.56
  47.8 1.4 subtract_convert_fusion.1
  49.2 0.8 fusion.31
  50.1 21.1 %all_gather.15 = bf16[256,1536]{1,0:T(8,128)(2,1)} all-gather(bf16[64,1536]{1,0:T(8,128)(2,1)} %param.11), channel_id=1, replica_groups=mesh['seq'=8,'mp'=4] {'mp'}, dimensions={0}, use_global_device_ids=true | all-gather | bytes 983040 | tf_op jit(solution)/shard_map/all_gather | solution.py:66
  71.1 1.0 reshape.282
  72.7 1.0 reshape.283
  74.5 1.3 copy.59
  75.8 1.8 all-gather.3.cloned.1.call-done
  77.6 16.0 %broadcast_in_dim.40 = f32[8192,4,128]{2,1,0:T(4,128)S(1)} broadcast(f32[8192,4]{1,0:T(8,128)} %copy.56), dimensions={0,1} | broadcast | bytes 16908288 | tf_op jit(solution)/shard_map/broadcast_in_dim | solution.py:41
  93.7 6.7 %fusion.6 = bf16[8192,512]{1,0:T(8,128)(2,1)} fusion(f32[1024,8,4,128]{3,2,1,0:T(4,128)S(1)} %bitcast.61, bf16[8192,512]{1,0:T(8,128)(2,1)S(1)} %copy-done.5), kind=kLoop, calls=%fused_computation.14 | loop fusion | flops 12582912 | bytes 33554432 | tf_op jit(solution)/shard_map/convert_element_type | solution.py:42
  100.4 77.9 %all-gather.5.cloned.1.call-done = bf16[1536,6144]{1,0:T(8,128)(2,1)} async-done(((bf16[192,6144]{1,0:T(8,128)(2,1)}), bf16[1536,6144]{1,0:T(8,128)(2,1)}) %all-gather.5.cloned.1.call-update) | async-done | bytes 18874384 | tf_op jit(solution)/shard_map/all_gather | solution.py:71
  178.3 12.7 %broadcast_in_dim.50 = f32[1536,48,128]{2,1,0:T(8,128)} broadcast(f32[1536,48]{1,0:T(8,128)S(1)} %copy.61), dimensions={0,1} | broadcast | bytes 38043648 | tf_op jit(solution)/shard_map/broadcast_in_dim | solution.py:41
  191.0 28.9 %fusion.12 = bf16[6144,256]{1,0:T(8,128)(2,1)S(1)} fusion(bf16[256,1536]{1,0:T(8,128)(2,1)S(1)} %copy-done.6, f32[192,8,48,128]{3,2,1,0:T(8,128)} %bitcast.60, bf16[1536,6144]{1,0:T(8,128)(2,1)} %all-gather.5.cloned.1.call-done), kind=kOutput, calls=%fused_computation.22 | convolution fusion | flops 4861722624 | bytes 60555264 | tf_op jit(solution)/shard_map/dot_general | solution.py:47
  219.9 1.8 slice_convert_fusion
  222.2 5.3 %convolution_convert_fusion = bf16[32,512,256]{2,1,0:T(8,128)(2,1)S(1)} fusion(bf16[32,256,512]{2,1,0:T(8,128)(2,1)} %bitcast.62, bf16[256,32,192]{0,2,1:T(8,128)(2,1)} %bitcast.65), kind=kOutput, calls=%fused_computation.23 | convolution fusion | flops 1077936128 | bytes 14680064 | tf_op jit(solution)/shard_map/thd,hdc->thc/dot_general | solution.py:85
  227.5 5.7 %fusion.7 = f32[256,256,32]{1,0,2:T(8,128)} fusion(bf16[32,512,256]{2,1,0:T(8,128)(2,1)S(1)} %convolution_convert_fusion, bf16[256,512]{0,1:T(8,128)(2,1)S(1)} %fusion.31), kind=kOutput, calls=%fused_computation.16 | convolution fusion | flops 2147483648 | bytes 17039360 | tf_op jit(solution)/shard_map/thc,kc->htk/dot_general | solution.py:126
  234.0 13.2 %fusion.28 = f32[1024,256,32]{1,0,2:T(8,128)} fusion(bf16[256,32,32]{0,2,1:T(8,128)(2,1)S(1)} %get-tuple-element.8, bf16[256,32,32]{0,2,1:T(8,128)(2,1)S(1)} %get-tuple-element.7, bf16[1024,64]{1,0:T(8,128)(2,1)S(1)} %copy-done.7), kind=kOutput, calls=%fused_computation.38 | convolution fusion | flops 1075838976 | bytes 34734080 | tf_op jit(solution)/shard_map/thr,kr->htk/dot_general | solution.py:129
  247.2 29.0 %fusion.54 = (f32[32,256]{1,0:T(8,128)S(1)}, f32[32,256,1024]{1,2,0:T(8,128)}) fusion(f32[1024,256,32]{1,0,2:T(8,128)} %fusion.28, bf16[1024,512,1]{1,0,2:T(8,128)(2,1)S(1)} %bitcast.67, bf16[32,512,256]{2,1,0:T(8,128)(2,1)} %copy-done.2, pred[1024]{0:T(1024)(128)(4,1)S(1)} %copy-done.10), kind=kOutput, calls=%fused_computation.98 | convolution fusion | flops 8623480832 | bytes 76579840 | tf_op jit(solution)/shard_map/thc,kc->htk/dot_general | solution.py:126
  276.3 8.2 %fusion.55 = (f32[32,256]{1,0:T(8,128)S(1)}, f32[32,256,256]{1,2,0:T(8,128)}) fusion(f32[256,256,32]{1,0,2:T(8,128)} %fusion.7, bf16[256,32,32]{0,2,1:T(8,128)(2,1)S(1)} %get-tuple-element.8, bf16[256,32,32]{0,2,1:T(8,128)(2,1)S(1)} %get-tuple-element.7, bf16[256,32]{0,1:T(8,128)(2,1)S(1)} %copy-done.9, bf16[256,32]{0,1:T(8,128)(2,1)S(1)} %get-tuple-element.9, ...), kind=kOutput, calls=%fused_computation.99 | convolution fusion | flops 278978560 | bytes 17956864 | tf_op jit(solution)/shard_map/thr,kr->htk/dot_general | solution.py:129
  284.5 14.3 %fusion.2 = f32[32,256]{1,0:T(8,128)S(1)} fusion(f32[32,256,256]{1,2,0:T(8,128)} %get-tuple-element.16, f32[32,256,1024]{1,2,0:T(8,128)} %get-tuple-element.14, f32[32,256]{1,0:T(8,128)S(1)} %reduce_max.22), kind=kLoop, calls=%fused_computation.10 | loop fusion | flops 31449088 | bytes 42008576 | tf_op jit(solution)/shard_map/reduce_sum | solution.py:143
  298.8 20.3 %fusion.19 = bf16[32,128,256]{2,1,0:T(8,128)(2,1)S(1)} fusion(f32[32,256,256]{1,2,0:T(8,128)} %get-tuple-element.16, f32[32,256,1024]{1,2,0:T(8,128)} %get-tuple-element.14, f32[32,256]{1,0:T(8,128)S(1)} %fusion.2, f32[32,256]{1,0:T(8,128)S(1)} %reduce_max.22, bf16[32,256,512]{2,1,0:T(8,128)(2,1)} %bitcast.63, bf16[256,512]{0,1:T(8,128)(2,1)S(1)} %fusion.31, ...), kind=kOutput, calls=%fused_computation.30 | convolution fusion | flops 11860967424 | bytes 49610752 | tf_op jit(solution)/shard_map/thc,hvc->thv/dot_general | solution.py:148
  319.1 2.9 copy.69
  (62 shorter events, 8.4 us)
Async XLA Ops:
  6.5 32.6 %copy-start = (bf16[16,64,512]{2,1,0:T(8,128)(2,1)S(1)}, bf16[16,64,512]{2,1,0:T(8,128)(2,1)}, u32[]{:S(2)}) copy-start(bf16[16,64,512]{2,1,0:T(8,128)(2,1)} %param.18) | copy-start | bytes 3145732
  6.5 31.7 %copy-start.12 = (f32[64,4]{0,1:T(4,128)S(1)}, f32[64,4]{0,1:T(4,128)}, u32[]{:S(2)}) copy-start(f32[64,4]{0,1:T(4,128)} %param.16) | copy-start | bytes 3076
  6.5 71.1 %all-gather.3.cloned.1.call-start = ((), (), s32[]{:S(2)}) async-start(), calls=%async_computation.2 | async-start | bytes 9437184 | tf_op jit(solution)/shard_map/all_gather | solution.py:73
  7.3 171.0 %all-gather.5.cloned.1.call-start = ((), (), s32[]{:S(2)}) async-start(), calls=%async_computation.3 | async-start | bytes 21233664 | tf_op jit(solution)/shard_map/all_gather | solution.py:71
  12.5 28.3 %all-to-all-start.1 = ((bf16[8,2,4096]{2,1,0:T(2,128)(2,1)}), bf16[8,2,4096]{2,1,0:T(2,128)(2,1)S(1)}, u32[]{:S(2)}, u32[]{:S(2)}) async-start(bf16[8,2,4096]{2,1,0:T(2,128)(2,1)} %reshape.281), calls=%async_computation.1 | async-start | bytes 262144 | tf_op jit(solution)/shard_map/all_to_all | solution.py:111
  40.7 33.0 %copy-start.11 = (s32[1024]{0:T(1024)}, s32[1024]{0:T(1024)S(1)}, u32[]{:S(2)}) copy-start(s32[1024]{0:T(1024)S(1)} %pad_clamp_fusion) | copy-start | bytes 12292
  40.8 4.0 %copy-start.8 = (bf16[8,2,4096]{2,1,0:T(2,128)(2,1)}, bf16[8,2,4096]{2,1,0:T(2,128)(2,1)S(1)}, u32[]{:S(2)}) copy-start(bf16[8,2,4096]{2,1,0:T(2,128)(2,1)S(1)} %all-to-all-done.1) | copy-start | bytes 393220
  40.8 33.0 %all-to-all-start = ((bf16[8,2,64,512]{3,2,1,0:T(8,128)(2,1)}), bf16[8,2,64,512]{3,2,1,0:T(8,128)(2,1)S(1)}, u32[]{:S(2)}, u32[]{:S(2)}) async-start(bf16[8,2,64,512]{3,2,1,0:T(8,128)(2,1)} %bitcast.2), calls=%async_computation | async-start | bytes 2097152 | tf_op jit(solution)/shard_map/all_to_all | solution.py:110
  77.6 16.1 %copy-start.5 = (bf16[8192,512]{1,0:T(8,128)(2,1)S(1)}, bf16[8192,512]{1,0:T(8,128)(2,1)}, u32[]{:S(2)}) copy-start(bf16[8192,512]{1,0:T(8,128)(2,1)} %all-gather.3.cloned.1.call-done) | copy-start | bytes 25165828
  100.4 90.6 %copy-start.6 = (bf16[256,1536]{1,0:T(8,128)(2,1)S(1)}, bf16[256,1536]{1,0:T(8,128)(2,1)}, u32[]{:S(2)}) copy-start(bf16[256,1536]{1,0:T(8,128)(2,1)} %all_gather.15) | copy-start | bytes 2359300
  219.9 2.3 copy-start.3
  227.5 6.2 %copy-start.2 = (bf16[32,512,256]{2,1,0:T(8,128)(2,1)}, bf16[32,512,256]{2,1,0:T(8,128)(2,1)S(1)}, u32[]{:S(2)}) copy-start(bf16[32,512,256]{2,1,0:T(8,128)(2,1)S(1)} %convolution_convert_fusion) | copy-start | bytes 25165828
  227.5 6.2 %copy-start.4 = (f32[256,32,64]{0,2,1:T(8,128)S(1)}, f32[256,32,64]{0,2,1:T(8,128)}, u32[]{:S(2)}) copy-start(f32[256,32,64]{0,2,1:T(8,128)} %slice_convert_fusion) | copy-start | bytes 6291460
  227.5 6.5 %copy-start.7 = (bf16[1024,64]{1,0:T(8,128)(2,1)S(1)}, bf16[1024,64]{1,0:T(8,128)(2,1)}, u32[]{:S(2)}) copy-start(bf16[1024,64]{1,0:T(8,128)(2,1)} %reshape.283) | copy-start | bytes 393220
  234.0 13.3 %copy-start.10 = (pred[1024]{0:T(1024)(128)(4,1)S(1)}, pred[1024]{0:T(1024)(128)(4,1)}, u32[]{:S(2)}) copy-start(pred[1024]{0:T(1024)(128)(4,1)} %iota_compare_fusion.5) | copy-start | bytes 3076
  247.2 29.0 %copy-start.9 = (bf16[256,32]{0,1:T(8,128)(2,1)S(1)}, bf16[256,32]{0,1:T(8,128)(2,1)}, u32[]{:S(2)}) copy-start(bf16[256,32]{0,1:T(8,128)(2,1)} %get-tuple-element.10) | copy-start | bytes 49156
  298.8 23.2 %copy-start.1 = (bf16[16,64,512]{2,1,0:T(8,128)(2,1)S(1)}, bf16[16,64,512]{2,1,0:T(8,128)(2,1)}, u32[]{:S(2)}) copy-start(bf16[16,64,512]{2,1,0:T(8,128)(2,1)} %param.18) | copy-start | bytes 3145732
Sparse Core Ops, SparseCore 0:
  9.2 68.3 all-gather.2
  79.5 98.7 all-gather.4
where the time goes:
time: 329 us
  matrix products  111 us (34%)
  waiting for transfers between devices  81.1 us (25%)
  local copies, waits for them, and re-layouts  45.9 us (14%)
  blocking collectives  36 us (11%)
  other arithmetic  32.5 us (10%)
  between operations  13.7 us (4%)
  starting transfers between devices  9.16 us (3%)
    all_gather x1, waiting for transfers between devices, body(): lax.all_gather(q_weight, 'seq', axis=0, tiled=True)  77.9 us
    dot_general x2, matrix products, score_keys(): jnp.einsum('thc,kc->htk', query_lat, keys_lat, preferred_element_type=jnp...  34.7 us
    dot_general x1, matrix products, add_rows(): return jnp.dot(query_rows, dense_rows, preferred_element_type=jnp.float32)  28.9 us
    broadcast_in_dim x2, local copies, waits for them, and re-layouts, dequantize_rows(): factors = jnp.repeat(per_row, BLOCK, axis=1)  28.7 us
    dot_general x2, matrix products, score_keys(): jnp.einsum('thr,kr->htk', query_rope, keys_rope, preferred_element_type=j...  21.4 us
    all_gather x1, blocking collectives, body(): lax.all_gather(query_latent, 'mp', axis=0, tiled=True)  21.1 us
    dot_general x1, matrix products, body(): jnp.einsum('thc,hvc->thv', mixed, value_weight, preferred_element_type=jn...  20.3 us
    all_gather x1, blocking collectives, body(): lax.all_gather(new_kv, 'mp', axis=0, tiled=True)  14.9 us
  transfers between devices with their start and end apart: 4, of which 2 were waited for; matrix products, arithmetic and copies ran while one was open for 14% of the time, Pallas kernels for 0%

commit v1 on v0

--- a/solution.py
+++ b/solution.py
@@ -1,8 +1,11 @@
+import functools
 import math
 
 import jax
 import jax.numpy as jnp
 from jax import lax
+from jax.experimental import pallas as pl
+from jax.experimental.pallas import tpu as pltpu
 from jax.sharding import PartitionSpec as P
 
 NOPE = 128
@@ -151,6 +154,477 @@
     return attended.reshape(tok_rows, head_count * VDIM)
 
 
+MESH = pl.DeviceIdType.MESH
+KEYW = LATENT + 2 * ROPE
+HEADW = NOPE + ROPE
+KV_UNITS = 4
+Q_UNITS = 8
+UNITS = KV_UNITS + Q_UNITS
+LANES = 9
+AHEAD = 3
+
+
+def fused_kernel(
+    query_ref,
+    new_ref,
+    pages_ref,
+    qw_ref,
+    kv_ref,
+    qs_ref,
+    ks_ref,
+    cos_ref,
+    sin_ref,
+    bias_ref,
+    out_ref,
+    q_all,
+    kv_all,
+    keys,
+    queries,
+    wq,
+    send_sem,
+    recv_sem,
+    page_send,
+    page_recv,
+    row_send,
+    row_recv,
+    own_sem,
+):
+    me = lax.axis_index("seq")
+    z = lax.axis_index("mp")
+    n_seq = pages_ref.shape[0]
+    n_mp = queries.shape[0] // query_ref.shape[0]
+    core = lax.rem(me, 2)
+    across = lax.rem(me // 2, 2)
+    down = me // 4
+    sib = me + 1 - 2 * core
+    xn = me + 2 - 4 * across
+    yn = me + 4 - 8 * down
+    dn = xn + 4 - 8 * down
+    sib_x = sib + 2 - 4 * across
+    sib_y = sib + 4 - 8 * down
+    sib_d = sib_x + 4 - 8 * down
+
+    q_rows = qw_ref.shape[0]
+    q_cols = qw_ref.shape[1] // Q_UNITS
+    kv_rows = kv_ref.shape[0]
+    kv_part = kv_rows // KV_UNITS
+    page_rows = pages_ref.shape[1]
+    prior = n_seq * page_rows
+    own_rows = query_ref.shape[0]
+    toks = queries.shape[0]
+
+    barrier = pltpu.get_barrier_semaphore()
+    for i in range(1, n_seq):
+        pl.semaphore_signal(
+            barrier, inc=1, device_id=(lax.rem(me + i, n_seq), z), device_id_type=MESH
+        )
+    for i in range(1, n_mp):
+        pl.semaphore_signal(
+            barrier, inc=1, device_id=(me, lax.rem(z + i, n_mp)), device_id_type=MESH
+        )
+    pl.semaphore_wait(barrier, n_seq + n_mp - 2)
+
+    def row_copies(i):
+        target = (me, lax.rem(z + i, n_mp))
+        return (
+            pltpu.make_async_remote_copy(
+                src_ref=query_ref,
+                dst_ref=queries.at[pl.ds(z * own_rows, own_rows)],
+                send_sem=row_send.at[2 * i],
+                recv_sem=row_recv.at[2 * i],
+                device_id=target,
+                device_id_type=MESH,
+            ),
+            pltpu.make_async_remote_copy(
+                src_ref=new_ref,
+                dst_ref=keys.at[pl.ds(prior + z * own_rows, own_rows)],
+                send_sem=row_send.at[2 * i + 1],
+                recv_sem=row_recv.at[2 * i + 1],
+                device_id=target,
+                device_id_type=MESH,
+            ),
+        )
+
+    def page_copy(i):
+        target = lax.rem(me + i, n_seq)
+        return pltpu.make_async_remote_copy(
+            src_ref=pages_ref.at[target],
+            dst_ref=keys.at[pl.ds(me * page_rows, page_rows)],
+            send_sem=page_send.at[i],
+            recv_sem=page_recv.at[i],
+            device_id=(target, z),
+            device_id_type=MESH,
+        )
+
+    def row_arrivals(i):
+        owner = lax.rem(z + n_mp - i, n_mp)
+        for kind, (buf, base) in enumerate(((queries, 0), (keys, prior))):
+            ref = buf.at[pl.ds(base + owner * own_rows, own_rows)]
+            pltpu.make_async_remote_copy(
+                src_ref=ref,
+                dst_ref=ref,
+                send_sem=row_send.at[2 * i + kind],
+                recv_sem=row_recv.at[2 * i + kind],
+                device_id=(me, owner),
+                device_id_type=MESH,
+            ).wait_recv()
+
+    def page_arrival(i):
+        owner = lax.rem(me + n_seq - i, n_seq)
+        ref = keys.at[pl.ds(owner * page_rows, page_rows)]
+        pltpu.make_async_remote_copy(
+            src_ref=ref,
+            dst_ref=ref,
+            send_sem=page_send.at[i],
+            recv_sem=page_recv.at[i],
+            device_id=(owner, z),
+            device_id_type=MESH,
+        ).wait_recv()
+
+    local = [
+        pltpu.make_async_copy(
+            query_ref, queries.at[pl.ds(z * own_rows, own_rows)], own_sem.at[Q_UNITS]
+        ),
+        pltpu.make_async_copy(
+            new_ref, keys.at[pl.ds(prior + z * own_rows, own_rows)], own_sem.at[Q_UNITS + 1]
+        ),
+        pltpu.make_async_copy(
+            pages_ref.at[me], keys.at[pl.ds(me * page_rows, page_rows)], own_sem.at[Q_UNITS + 2]
+        ),
+        pltpu.make_async_copy(
+            kv_ref, kv_all.at[pl.ds(me * kv_rows, kv_rows)], own_sem.at[Q_UNITS + 3]
+        ),
+    ]
+
+    def own_panel(k):
+        return pltpu.make_async_copy(
+            qw_ref.at[:, pl.ds(pl.multiple_of(k * q_cols, 128), q_cols)],
+            q_all.at[k, pl.ds(me * q_rows, q_rows)],
+            own_sem.at[k],
+        )
+
+    def place(is_q, owner, unit, half):
+        if is_q:
+            step = q_rows // 2
+            start, size = (owner * q_rows, q_rows) if half is None else (
+                owner * q_rows + half * step, step)
+            return q_all.at[unit - KV_UNITS, pl.ds(start, size)]
+        step = kv_part // 2
+        base = owner * kv_rows + unit * kv_part
+        start, size = (base, kv_part) if half is None else (base + half * step, step)
+        return kv_all.at[pl.ds(start, size)]
+
+    def own_source(is_q, unit):
+        if is_q:
+            first = pl.multiple_of((unit - KV_UNITS) * q_cols, 128)
+            return qw_ref.at[:, pl.ds(first, q_cols)]
+        return kv_ref.at[pl.ds(unit * kv_part, kv_part)]
+
+    def link(src, dst, unit, lane, target):
+        at = unit * LANES + lane
+        return pltpu.make_async_remote_copy(
+            src_ref=src,
+            dst_ref=dst,
+            send_sem=send_sem.at[at],
+            recv_sem=recv_sem.at[at],
+            device_id=(target, z),
+            device_id_type=MESH,
+        )
+
+    def arrived(is_q, unit, lane, owner, half, sender):
+        ref = place(is_q, owner, unit, half)
+        link(ref, ref, unit, lane, sender).wait_recv()
+
+    def forward(is_q, unit, lane, owner, half, target):
+        ref = place(is_q, owner, unit, half)
+        link(ref, ref, unit, lane, target).start()
+
+    def each_kind(low, high, unit, act):
+        @pl.when((unit >= low) & (unit < KV_UNITS))
+        def _():
+            act(False)
+
+        @pl.when((unit >= KV_UNITS) & (unit < high))
+        def _():
+            act(True)
+
+    def send_own(unit):
+        def act(is_q):
+            src = own_source(is_q, unit)
+            dst = place(is_q, me, unit, None)
+            link(src, dst, unit, 0, xn).start()
+            link(src, dst, unit, 1, yn).start()
+            link(src, dst, unit, 4, sib).start()
+
+        each_kind(0, UNITS, unit, act)
+
+    def relay(unit):
+        def act(is_q):
+            arrived(is_q, unit, 0, xn, None, xn)
+            forward(is_q, unit, 2, xn, 0, yn)
+            forward(is_q, unit, 5, xn, None, sib)
+            arrived(is_q, unit, 1, yn, None, yn)
+            forward(is_q, unit, 3, yn, 1, xn)
+            forward(is_q, unit, 6, yn, None, sib)
+
+        each_kind(0, UNITS, unit, act)
+
+    def share(unit):
+        def act(is_q):
+            arrived(is_q, unit, 2, dn, 0, yn)
+            forward(is_q, unit, 7, dn, 0, sib)
+            arrived(is_q, unit, 3, dn, 1, xn)
+            forward(is_q, unit, 8, dn, 1, sib)
+
+        each_kind(0, UNITS, unit, act)
+
+    def collect(unit):
+        def act(is_q):
+            arrived(is_q, unit, 4, sib, None, sib)
+            arrived(is_q, unit, 5, sib_x, None, sib)
+            arrived(is_q, unit, 6, sib_y, None, sib)
+            arrived(is_q, unit, 7, sib_d, 0, sib)
+            arrived(is_q, unit, 8, sib_d, 1, sib)
+
+        each_kind(0, UNITS, unit, act)
+
+    def sent(unit):
+        def act(is_q):
+            whole = place(is_q, me, unit, None)
+            part = place(is_q, me, unit, 0)
+            for lane in (0, 1, 4, 5, 6):
+                link(whole, whole, unit, lane, sib).wait_send()
+            for lane in (2, 3, 7, 8):
+                link(part, part, unit, lane, sib).wait_send()
+
+        each_kind(0, UNITS, unit, act)
+
+    lane_id = lax.broadcasted_iota(jnp.int32, (toks, 2 * ROPE), 1)
+    low_half = lane_id < ROPE
+    low_quarter = lax.rem(lane_id, ROPE) < ROPE // 2
+    scale = math.log2(math.e) / math.sqrt(NOPE + ROPE)
+
+    def scale_row(ref, row, first, count):
+        return jnp.concatenate(
+            [jnp.full((1, BLOCK), ref[row, first + b], jnp.float32) for b in range(count)], axis=1
+        )
+
+    def two_heads(pair, unit, side):
+        for b in range(wq.shape[0] // BLOCK):
+            rows = slice(b * BLOCK, (b + 1) * BLOCK)
+            block = q_all[unit, rows, side * 2 * HEADW : (side + 1) * 2 * HEADW]
+            wq[rows, :] = (
+                block.astype(jnp.float32) * scale_row(qs_ref, b, 3 * pair, 3)
+            ).astype(jnp.bfloat16)
+        q = jnp.dot(queries[...], wq[...], preferred_element_type=jnp.float32)
+        q = q.astype(jnp.bfloat16).astype(jnp.float32)
+        mid, end = q[:, NOPE : 2 * NOPE], q[:, 2 * NOPE :]
+        nope = (
+            q[:, :NOPE].astype(jnp.bfloat16),
+            jnp.where(low_half, pltpu.roll(mid, ROPE, 1), pltpu.roll(end, ROPE, 1)).astype(
+                jnp.bfloat16
+            ),
+        )
+        flat = jnp.where(low_half, mid, end)
+        swapped = jnp.where(low_quarter, pltpu.roll(flat, 96, 1), pltpu.roll(flat, 32, 1))
+        turned = flat * cos_ref[...] + swapped * sin_ref[...]
+        ropes = (turned.astype(jnp.bfloat16), pltpu.roll(turned, ROPE, 1).astype(jnp.bfloat16))
+        row_id = lax.broadcasted_iota(jnp.int32, (toks, toks), 0)
+        col_id = lax.broadcasted_iota(jnp.int32, (toks, toks), 1)
+        causal = col_id <= row_id
+        outs = []
+        for side_head in range(2):
+            head = 2 * pair + side_head
+            first = pl.multiple_of(head * 2 * BLOCK, 2 * BLOCK)
+            wk = (
+                kv_all[pl.ds(first, BLOCK), :].astype(jnp.float32)
+                * scale_row(ks_ref, 2 * head, 0, LATENT // BLOCK)
+            ).astype(jnp.bfloat16)
+            wv = (
+                kv_all[pl.ds(first + BLOCK, BLOCK), :].astype(jnp.float32)
+                * scale_row(ks_ref, 2 * head + 1, 0, LATENT // BLOCK)
+            ).astype(jnp.bfloat16)
+            lat = jnp.dot(nope[side_head], wk, preferred_element_type=jnp.float32).astype(
+                jnp.bfloat16
+            )
+            full = jnp.concatenate([lat, ropes[side_head]], axis=1)
+            dims = (((1,), (1,)), ((), ()))
+            s = lax.dot_general(full, keys[...], dims, preferred_element_type=jnp.float32)
+            s_old = s[:, :prior] + bias_ref[...]
+            s_new = jnp.where(causal, s[:, prior:], -jnp.inf)
+            s = jnp.concatenate([s_old, s_new], axis=1)
+            top = jnp.max(s, axis=1, keepdims=True)
+            e = jnp.exp2((s - top) * scale)
+            w = (e * (1.0 / jnp.sum(e, axis=1, keepdims=True))).astype(jnp.bfloat16)
+            mixed = jnp.dot(w, keys[:, :LATENT], preferred_element_type=jnp.float32).astype(
+                jnp.bfloat16
+            )
+            outs.append(
+                lax.dot_general(mixed, wv, dims, preferred_element_type=jnp.float32).astype(
+                    jnp.bfloat16
+                )
+            )
+        out_ref[:, pl.ds(pl.multiple_of(pair * 2 * VDIM, 2 * VDIM), 2 * VDIM)] = jnp.concatenate(
+            outs, axis=1
+        )
+
+    for i in range(1, n_mp):
+        for copy in row_copies(i):
+            copy.start()
+    for i in range(1, n_seq):
+        page_copy(i).start()
+    for u in range(AHEAD):
+        send_own(jnp.int32(u))
+    for copy in local:
+        copy.start()
+    for k in range(Q_UNITS):
+        own_panel(k).start()
+
+    def step(t, carry):
+        relay(t)
+        send_own(t + AHEAD)
+        share(t - 1)
+        collect(t - 2)
+
+        @pl.when(t - 2 == KV_UNITS)
+        def _():
+            for i in range(1, n_mp):
+                row_arrivals(i)
+            for i in range(1, n_seq):
+                page_arrival(i)
+            for copy in local:
+                copy.wait()
+
+        @pl.when(t - 2 >= KV_UNITS)
+        def _():
+            k = t - 2 - KV_UNITS
+            own_panel(k).wait()
+            two_heads(2 * k, k, 0)
+            two_heads(2 * k + 1, k, 1)
+
+        return carry
+
+    lax.fori_loop(0, UNITS + 2, step, 0)
+
+    for i in range(1, n_mp):
+        for copy in row_copies(i):
+            copy.wait_send()
+    for i in range(1, n_seq):
+        page_copy(i).wait_send()
+
+    def drain(u, carry):
+        sent(u)
+        return carry
+
+    lax.fori_loop(0, UNITS, drain, 0)
+
+
+def fused_body(
+    query_latent,
+    new_kv,
+    q_weight,
+    q_scales,
+    kv_weight,
+    kv_scales,
+    kv_gain,
+    pool_latent,
+    pool_rope,
+    page_table,
+    prior_len,
+):
+    seq_count = lax.axis_size("seq")
+    mp_count = lax.axis_size("mp")
+    own_index = lax.axis_index("seq")
+    mp_index = lax.axis_index("mp")
+    own_rows = query_latent.shape[0]
+    toks = own_rows * mp_count
+    page_count = page_table.shape[1]
+    pool_count, page_len = pool_latent.shape[:2]
+    length = lax.dynamic_index_in_dim(prior_len, own_index, 0, keepdims=False)
+    cosine, sine = rope_tables(length + jnp.arange(toks, dtype=jnp.int32))
+    cos_table = jnp.tile(cosine, (1, 4))
+    sin_table = jnp.tile(jnp.concatenate([-sine, sine], axis=1), (1, 2))
+
+    first = mp_index * own_rows
+    own_cos = lax.dynamic_slice_in_dim(cosine, first, own_rows, 0)
+    own_sin = lax.dynamic_slice_in_dim(sine, first, own_rows, 0)
+    latent_part = new_kv[:, :LATENT].astype(jnp.float32)
+    inv_rms = lax.rsqrt(jnp.mean(latent_part * latent_part, axis=-1, keepdims=True) + NORM_EPS)
+    new_lat = latent_part * inv_rms * kv_gain[None, :]
+    new_rope = rotate(new_kv[:, LATENT:].astype(jnp.float32), own_cos, own_sin)
+    new_keys = jnp.concatenate([new_lat, new_rope, jnp.zeros_like(new_rope)], axis=1).astype(
+        jnp.bfloat16
+    )
+
+    holders = page_table // pool_count
+    pool_slots = page_table % pool_count
+    earlier = jnp.arange(page_count)[None, :] < jnp.arange(page_count)[:, None]
+    same_holder = holders[:, :, None] == holders[:, None, :]
+    page_ranks = jnp.sum(jnp.where(same_holder & earlier[None], 1, 0), axis=2)
+    capacity = (page_count + seq_count - 1) // seq_count
+    wanted = (holders[:, None, :] == own_index) & (
+        page_ranks[:, None, :] == jnp.arange(capacity)[None, :, None]
+    )
+    send_slot = jnp.sum(jnp.where(wanted, pool_slots[:, None, :], 0), axis=2).reshape(-1)
+    rope_rows = pool_rope.reshape(pool_count, page_len, ROPE)
+    pool_keys = jnp.concatenate([pool_latent, rope_rows, jnp.zeros_like(rope_rows)], axis=2)
+    pages = pool_keys[send_slot].reshape(seq_count, capacity * page_len, KEYW)
+
+    own_place = lax.dynamic_index_in_dim(holders * capacity + page_ranks, own_index, 0, False)
+    at_slot = own_place[None, :] == jnp.arange(seq_count * capacity)[:, None]
+    slot_page = jnp.sum(jnp.where(at_slot, jnp.arange(page_count)[None, :], 0), axis=1)
+    slot_page = jnp.where(jnp.any(at_slot, axis=1), slot_page, page_count)
+    token = slot_page[:, None] * page_len + jnp.arange(page_len)[None, :]
+    seen = token < jnp.minimum(length, page_count * page_len)
+    bias = jnp.where(seen, 0.0, -jnp.inf).astype(jnp.float32).reshape(1, -1)
+
+    prior = seq_count * capacity * page_len
+    heads = q_weight.shape[1] // HEADW
+    anywhere = pl.BlockSpec(memory_space=pl.ANY)
+    vmem = pl.BlockSpec(memory_space=pltpu.VMEM)
+    smem = pl.BlockSpec(memory_space=pltpu.SMEM)
+    return pl.pallas_call(
+        fused_kernel,
+        out_shape=jax.ShapeDtypeStruct((toks, heads * VDIM), jnp.bfloat16),
+        in_specs=[anywhere] * 5 + [smem] * 2 + [vmem] * 3,
+        out_specs=vmem,
+        scratch_shapes=[
+            pltpu.VMEM(
+                (Q_UNITS, q_weight.shape[0] * seq_count, q_weight.shape[1] // Q_UNITS),
+                jnp.bfloat16,
+            ),
+            pltpu.VMEM((kv_weight.shape[0] * seq_count, LATENT), jnp.bfloat16),
+            pltpu.VMEM((prior + toks, KEYW), jnp.bfloat16),
+            pltpu.VMEM((toks, query_latent.shape[1]), jnp.bfloat16),
+            pltpu.VMEM((q_weight.shape[0] * seq_count, 2 * HEADW), jnp.bfloat16),
+            pltpu.SemaphoreType.DMA((UNITS * LANES,)),
+            pltpu.SemaphoreType.DMA((UNITS * LANES,)),
+            pltpu.SemaphoreType.DMA((seq_count,)),
+            pltpu.SemaphoreType.DMA((seq_count,)),
+            pltpu.SemaphoreType.DMA((2 * mp_count,)),
+            pltpu.SemaphoreType.DMA((2 * mp_count,)),
+            pltpu.SemaphoreType.DMA((Q_UNITS + 4,)),
+        ],
+        compiler_params=pltpu.CompilerParams(
+            collective_id=0, has_side_effects=True, vmem_limit_bytes=56 * 1024 * 1024
+        ),
+        cost_estimate=pl.CostEstimate(
+            flops=30 * 10**9, bytes_accessed=10**7, transcendentals=10**7
+        ),
+    )(
+        query_latent,
+        new_keys,
+        pages,
+        q_weight,
+        kv_weight,
+        q_scales,
+        kv_scales,
+        cos_table,
+        sin_table,
+        bias,
+    )
+
+
 def solution(mesh):
     in_specs = (
         P(("seq", "mp"), None),
@@ -166,4 +640,11 @@
         P(),
     )
     out_specs = P("seq", "mp")
-    return jax.shard_map(body, mesh=mesh, in_specs=in_specs, out_specs=out_specs, check_vma=False)
+    fused = mesh.shape["seq"] == 8 and mesh.shape["mp"] == 4
+    return jax.shard_map(
+        fused_body if fused else body,
+        mesh=mesh,
+        in_specs=in_specs,
+        out_specs=out_specs,
+        check_vma=False,
+    )

time: 329 us -> 182 us (0.55)
  Pallas kernels: 0 us -> 163 us
  matrix products: 111 us -> 0 us
  waiting for transfers between devices: 81.1 us -> 0 us
  blocking collectives: 36 us -> 0 us
  local copies, waits for them, and re-layouts: 45.9 us -> 11.4 us
  other arithmetic: 32.5 us -> 7.18 us
  between operations: 13.7 us -> 0.79 us
  starting transfers between devices: 9.16 us -> 0 us
    pallas_call x0 -> x1, Pallas kernels: none -> 163 us  [fused_body(): pl.pallas_call(fused_kernel, out_shape=jax.ShapeDtypeStruct((toks, heads...]
    dot_general x7 -> x0, matrix products: 111 us -> none  [the longest x2 34.7 us: score_keys(): jnp.einsum('thc,kc->htk', query_lat, keys_lat, preferred_element_type=jnp...]
    all_gather x2 -> x0, waiting for transfers between devices: 79.7 us -> none  [the longest x1 77.9 us: body(): lax.all_gather(q_weight, 'seq', axis=0, tiled=True)]
    all_gather x2 -> x0, blocking collectives: 36 us -> none  [the longest x1 21.1 us: body(): lax.all_gather(query_latent, 'mp', axis=0, tiled=True)]
    broadcast_in_dim x2 -> x1, local copies, waits for them, and re-layouts: 28.7 us -> 0.01 us  [fused_body(): jnp.zeros_like(new_rope)]
    reduce_sum x6 -> x4, other arithmetic: 16.8 us -> 1.5 us  [the longest x1 0.95 us: fused_body(): jnp.mean(latent_part * latent_part, axis=-1, keepdims=True) + NORM_EPS]
    all_to_all x2 -> x0, starting transfers between devices: 9.12 us -> none  [the longest x1 5.17 us: body(): lax.all_to_all(send_rope, 'seq', split_axis=0, concat_axis=0, tiled=True)]
    convert_element_type x6 -> x1, other arithmetic: 9.5 us -> 0.72 us  [fused_body(): new_rope = rotate(new_kv[:, LATENT:].astype(jnp.float32), own_cos, own_sin)]
  transfers between devices with their start and end apart: 4 -> 0, of which waited for: 2 -> 0; matrix products, arithmetic and copies ran while one was open for 14% -> 0% of each run, Pallas kernels for 0% -> 0%
where the time goes in v1:
time: 182 us
  Pallas kernels  163 us (90%)
  local copies, waits for them, and re-layouts  11.4 us (6%)
  other arithmetic  7.18 us (4%)
    pallas_call x1, Pallas kernels, fused_body(): pl.pallas_call(fused_kernel, out_shape=jax.ShapeDtypeStruct((toks, heads...  163 us
    unnamed x4, local copies, waits for them, and re-layouts  4.52 us

profile of v1, /device:TPU:0, one launch (start us, length us, event | category | flops | bytes accessed | tf_op | source)
XLA Modules:
  0.0 182.0 jit_solution(3053875624663816598)
XLA Ops:
  0.0 1.2 dynamic_slice.14
  1.9 0.6 add_convert_fusion.1
  2.5 1.0 fusion
  3.5 0.1 pad.8.clone
  3.6 0.7 add_select_fusion
  4.3 0.7 broadcast_compare_fusion
  5.0 0.3 select_reduce_fusion
  5.3 0.2 select_reduce_fusion.2
  5.5 0.1 select_reduce_fusion.1
  5.6 0.1 fusion.4
  5.7 0.1 copy.25
  5.8 0.1 reshape.150
  5.9 0.1 fusion.6
  6.0 0.7 select_n.76.bias_ref
  6.7 1.4 copy.28.ks_ref
  8.0 0.7 slice_convert_fusion
  8.8 0.9 fusion.2
  9.7 0.0 copy-start
  9.7 1.3 reshape.149
  11.0 0.5 fusion.3
  11.5 0.1 subtract_convert_fusion
  11.6 0.1 pad_maximum_fusion
  11.7 0.1 copy.27
  11.8 0.7 maximum_maximum_fusion.1.new_ref
  12.5 0.1 copy.26
  12.6 0.7 copy.30.sin_ref
  13.4 0.8 copy.29.cos_ref
  14.1 0.0 copy-done
  14.1 0.3 maximum_maximum_fusion
  14.4 1.8 gather_fusion
  16.2 162.6 %shard_map.109 = bf16[256,4096]{1,0:T(8,128)(2,1)} custom-call(bf16[64,1536]{1,0:T(8,128)(2,1)} %query_ref.1, bf16[64,640]{1,0:T(8,128)(2,1)} %maximum_maximum_fusion.1.new_ref, bf16[8,128,640]{2,1,0:T(8,128)(2,1)} %bitcast.8, bf16[192,6144]{1,0:T(8,128)(2,1)} %qw_ref.1, bf16[1024,512]{1,0:T(8,128)(2,1)} %kv_ref.1, f32[12,48]{1,0:T(8,128)} %qs_ref.1, ...), custom_call_target="tpu_custom_call" | custom-call | flops 30000001024 | bytes 10000000 | tf_op jit(solution)/shard_map/pallas_call | solution.py:586
  178.9 3.1 %copy.32 = bf16[256,4096]{1,0:T(8,128)(2,1)} copy(bf16[256,4096]{1,0:T(8,128)(2,1)} %shard_map.109) | data formatting | bytes 4194304
  (11 shorter events, 0.1 us)
Async XLA Ops:
  9.7 4.4 %copy-start = (bf16[16,64,512]{2,1,0:T(8,128)(2,1)S(1)}, bf16[16,64,512]{2,1,0:T(8,128)(2,1)}, u32[]{:S(2)}) copy-start(bf16[16,64,512]{2,1,0:T(8,128)(2,1)} %param.18) | copy-start | bytes 3145732

commit v2 on v1

--- a/solution.py
+++ b/solution.py
@@ -433,6 +433,7 @@
         col_id = lax.broadcasted_iota(jnp.int32, (toks, toks), 1)
         causal = col_id <= row_id
         outs = []
+        scored = []
         for side_head in range(2):
             head = 2 * pair + side_head
             first = pl.multiple_of(head * 2 * BLOCK, 2 * BLOCK)
@@ -450,11 +451,14 @@
             full = jnp.concatenate([lat, ropes[side_head]], axis=1)
             dims = (((1,), (1,)), ((), ()))
             s = lax.dot_general(full, keys[...], dims, preferred_element_type=jnp.float32)
+            scored.append((s, wv))
+        for s, wv in scored:
             s_old = s[:, :prior] + bias_ref[...]
             s_new = jnp.where(causal, s[:, prior:], -jnp.inf)
-            s = jnp.concatenate([s_old, s_new], axis=1)
-            top = jnp.max(s, axis=1, keepdims=True)
-            e = jnp.exp2((s - top) * scale)
+            top = jnp.maximum(
+                jnp.max(s_old, axis=1, keepdims=True), jnp.max(s_new, axis=1, keepdims=True)
+            )
+            e = jnp.exp2((jnp.concatenate([s_old, s_new], axis=1) - top) * scale)
             w = (e * (1.0 / jnp.sum(e, axis=1, keepdims=True))).astype(jnp.bfloat16)
             mixed = jnp.dot(w, keys[:, :LATENT], preferred_element_type=jnp.float32).astype(
                 jnp.bfloat16
@@ -484,9 +488,9 @@
         relay(t)
         send_own(t + AHEAD)
         share(t - 1)
-        collect(t - 2)
-
-        @pl.when(t - 2 == KV_UNITS)
+        collect(t - 1)
+
+        @pl.when(t - 1 == KV_UNITS)
         def _():
             for i in range(1, n_mp):
                 row_arrivals(i)
@@ -495,16 +499,16 @@
             for copy in local:
                 copy.wait()
 
-        @pl.when(t - 2 >= KV_UNITS)
+        @pl.when(t - 1 >= KV_UNITS)
         def _():
-            k = t - 2 - KV_UNITS
+            k = t - 1 - KV_UNITS
             own_panel(k).wait()
             two_heads(2 * k, k, 0)
             two_heads(2 * k + 1, k, 1)
 
         return carry
 
-    lax.fori_loop(0, UNITS + 2, step, 0)
+    lax.fori_loop(0, UNITS + 1, step, 0)
 
     for i in range(1, n_mp):
         for copy in row_copies(i):

time: 182 us -> 172 us (0.945)
  Pallas kernels: 163 us -> 152 us
    pallas_call x1, Pallas kernels: 163 us -> 152 us  [fused_body(): pl.pallas_call(fused_kernel, out_shape=jax.ShapeDtypeStruct((toks, heads...]
where the time goes in v2:
time: 172 us
  Pallas kernels  152 us (88%)
  local copies, waits for them, and re-layouts  11.4 us (7%)
  other arithmetic  7.18 us (4%)
    pallas_call x1, Pallas kernels, fused_body(): pl.pallas_call(fused_kernel, out_shape=jax.ShapeDtypeStruct((toks, heads...  152 us
    unnamed x4, local copies, waits for them, and re-layouts  4.52 us

profile of v2, /device:TPU:0, one launch (start us, length us, event | category | flops | bytes accessed | tf_op | source)
XLA Modules:
  0.0 171.7 jit_solution(6199308738765602359)
XLA Ops:
  0.0 1.2 dynamic_slice.14
  1.9 0.6 add_convert_fusion.1
  2.5 1.0 fusion
  3.5 0.1 pad.8.clone
  3.6 0.7 add_select_fusion
  4.3 0.7 broadcast_compare_fusion
  5.0 0.3 select_reduce_fusion
  5.3 0.2 select_reduce_fusion.2
  5.5 0.1 select_reduce_fusion.1
  5.6 0.1 fusion.4
  5.7 0.1 copy.25
  5.8 0.1 reshape.150
  5.9 0.1 fusion.6
  6.0 0.7 select_n.76.bias_ref
  6.7 1.4 copy.28.ks_ref
  8.0 0.7 slice_convert_fusion
  8.8 0.9 fusion.2
  9.7 0.0 copy-start
  9.7 1.3 reshape.149
  11.0 0.5 fusion.3
  11.5 0.1 subtract_convert_fusion
  11.6 0.1 pad_maximum_fusion
  11.7 0.1 copy.27
  11.8 0.7 maximum_maximum_fusion.1.new_ref
  12.5 0.1 copy.26
  12.6 0.7 copy.30.sin_ref
  13.4 0.8 copy.29.cos_ref
  14.1 0.0 copy-done
  14.1 0.3 maximum_maximum_fusion
  14.4 1.8 %gather_fusion = bf16[16,64,640]{2,1,0:T(8,128)(2,1)} fusion(bf16[16,64,640]{2,1,0:T(8,128)(2,1)S(1)} %maximum_maximum_fusion, s32[1024]{0:T(1024)S(1)} %pad_clamp_fusion), kind=kCustom, calls=%fused_computation | custom fusion | bytes 2621504 | tf_op jit(solution)/shard_map/gather | solution.py:575
  16.2 152.4 %shard_map.109 = bf16[256,4096]{1,0:T(8,128)(2,1)} custom-call(bf16[64,1536]{1,0:T(8,128)(2,1)} %query_ref.1, bf16[64,640]{1,0:T(8,128)(2,1)} %maximum_maximum_fusion.1.new_ref, bf16[8,128,640]{2,1,0:T(8,128)(2,1)} %bitcast.8, bf16[192,6144]{1,0:T(8,128)(2,1)} %qw_ref.1, bf16[1024,512]{1,0:T(8,128)(2,1)} %kv_ref.1, f32[12,48]{1,0:T(8,128)} %qs_ref.1, ...), custom_call_target="tpu_custom_call" | custom-call | flops 30000001024 | bytes 10000000 | tf_op jit(solution)/shard_map/pallas_call | solution.py:590
  168.6 3.1 %copy.32 = bf16[256,4096]{1,0:T(8,128)(2,1)} copy(bf16[256,4096]{1,0:T(8,128)(2,1)} %shard_map.109) | data formatting | bytes 4194304
  (11 shorter events, 0.1 us)
Async XLA Ops:
  9.7 4.4 %copy-start = (bf16[16,64,512]{2,1,0:T(8,128)(2,1)S(1)}, bf16[16,64,512]{2,1,0:T(8,128)(2,1)}, u32[]{:S(2)}) copy-start(bf16[16,64,512]{2,1,0:T(8,128)(2,1)} %param.18) | copy-start | bytes 3145732
